TPU v7x, 32 devices: a whole 2x2x4 slice. The times are simulated.
32 devices in a mesh: groups: 2 (over x), slab: 16 (over z, y, core).
Axes of the slice: x: 2, y: 2, z: 4, core: 2. Of those that a mesh axis runs over, the one named last changes fastest.
Arguments:
- mode_shapes: float32 [16384, 192], P(('groups', 'slab')), parts along dimension 0, may hold values from -6 to 6
- wall_coupling: float32 [16384, 15], P(('groups', 'slab')), parts along dimension 0, may hold values from -3.5 to 3.5
- owner_dev: int32 [16384, 1], P(('groups', 'slab')), parts along dimension 0, may hold values from 0 to 15; in each aligned block of 512 rows (0 to 511, 512 to 1023, ...) at most 64 rows name the same one
- owner_cell: int32 [16384], P(('groups', 'slab')), parts along dimension 0, may hold values from 0 to 2047
- neighbours: int32 [6, 65536], P(None, ('groups', 'slab')), parts along dimension 1, may hold values from -1 to 32767, as said below
- coupling_blocks: float32 [6, 5, 5, 65536], P(None, None, None, ('groups', 'slab')), parts along dimension 3, may hold values from -0.3 to 0.3
- inv_blocks: float32 [5, 5, 65536], P(None, None, ('groups', 'slab')), parts along dimension 2, may hold values from -0.9 to 3, as said below
Outputs:
- modes_basis: float32 [5, 64, 65536], P(None, None, ('groups', 'slab')), parts along dimension 2
- factor: float32 [128, 64], P('groups'), parts along dimension 0
There are 2 independent parts, one for each index of `groups`. A program takes and returns all parts, laid end to end along the dimension named above; each array names one. Nothing has to cross between parts.
Inputs may be any that keep to these rules, and one draw needn't show every extreme that they name: `owner_dev`: in the rows of one slab device at most 64 shell nodes name the same slab, a bound that some of them reach. `neighbours`: A filled slot of cell c names a cell whose number differs from c by 1 to 256. `inv_blocks`: each block has a positive diagonal entry shared by its five diagonal places and off-diagonal entries of at most 0.3 times it in magnitude.
All inputs are finite; a program needn't handle non-finite values.
Results may differ from a plain program's by a relative error of at most 0.0003.
Values sent between devices are 32-bit elements; how exact they have to be, the bound alone decides.
No kernel may reach another device: no remote copies, remote signals or barrier semaphores. Data moves between devices by JAX's collectives and lax.ppermute only.
A program may use at most 192 MiB of HBM per device.

v0:
```python
import math
import jax
import jax.numpy as jnp
from jax import lax
from jax.sharding import PartitionSpec as P

VARS = 5
NBR = 6
SWEEPS = 2


def with_halo(x, sides, width):
    for axis, dim in sides:
        count, length = (lax.axis_size(axis), x.shape[dim])
        up = [(i, (i + 1) % count) for i in range(count - 1)]
        down = [(j, i) for i, j in up]
        last = lax.slice_in_dim(x, length - width, length, axis=dim)
        first = lax.slice_in_dim(x, 0, width, axis=dim)
        before = lax.ppermute(last, axis, up)
        after = lax.ppermute(first, axis, down)
        x = jnp.concatenate([before, x, after], axis=dim)
    return x


def apply_blocks(blocks, field_in):
    rows_out = []
    for out_var in range(field_in.shape[0]):
        summed = blocks[out_var, 0][None, :] * field_in[0]
        for in_var in range(1, field_in.shape[0]):
            summed = summed + blocks[out_var, in_var][None, :] * field_in[in_var]
        rows_out.append(summed)
    return jnp.stack(rows_out)


def couple(weights, shapes):
    node_count = weights.shape[0]
    modes_total = shapes.shape[1] // 3
    weights_split = weights.reshape(node_count, -1, 3)
    shapes_split = shapes.reshape(node_count, 3, modes_total)
    summed = weights_split[:, :, 0, None] * shapes_split[:, None, 0, :]
    for component in range(1, 3):
        summed = summed + weights_split[:, :, component, None] * shapes_split[:, None, component, :]
    return summed.reshape(node_count, -1)


def gram_matrix(left_field, right_field):
    return jnp.einsum("vpc,vqc->pq", left_field, right_field, precision=lax.Precision.HIGHEST)


def combine(coeffs, field_in):
    return jnp.einsum("pq,vpc->vqc", coeffs, field_in, precision=lax.Precision.HIGHEST)


def cholesky_upper(gram):
    order = gram.shape[0]
    places = jnp.arange(order, dtype=jnp.int32)

    def column_step(column_at, lower):
        row_now = lax.dynamic_index_in_dim(lower, column_at, 0, keepdims=False)
        target = lax.dynamic_index_in_dim(gram, column_at, 1, keepdims=False)
        reduced = target - jnp.dot(lower, row_now, precision=lax.Precision.HIGHEST)
        pivot = jnp.sqrt(lax.dynamic_index_in_dim(reduced, column_at, 0, keepdims=False))
        column = jnp.where(
            places > column_at, reduced / pivot, jnp.where(places == column_at, pivot, 0.0)
        )
        return jnp.where(places[None, :] == column_at, column[:, None], lower)

    lower = lax.fori_loop(0, order, column_step, jnp.zeros((order, order), jnp.float32))
    return lower.T


def upper_inverse(upper):
    lower = upper.T
    order = lower.shape[0]
    places = jnp.arange(order, dtype=jnp.int32)
    identity = jnp.eye(order, dtype=jnp.float32)

    def row_step(row_at, inverse):
        lower_row = lax.dynamic_index_in_dim(lower, row_at, 0, keepdims=False)
        pivot = lax.dynamic_index_in_dim(lower_row, row_at, 0, keepdims=False)
        earlier = jnp.where(places < row_at, lower_row, 0.0)
        unit_row = lax.dynamic_index_in_dim(identity, row_at, 0, keepdims=False)
        new_row = (unit_row - jnp.dot(earlier, inverse, precision=lax.Precision.HIGHEST)) / pivot
        return jnp.where(places[:, None] == row_at, new_row[None, :], inverse)

    inverse = lax.fori_loop(0, order, row_step, jnp.zeros((order, order), jnp.float32))
    return inverse.T


def local(
    mode_shapes, wall_coupling, owner_dev, owner_cell, neighbours, coupling_blocks, inv_blocks
):
    devices_slab = lax.axis_size("slab")
    cell_count = inv_blocks.shape[2]
    node_count = mode_shapes.shape[0]
    modes_total = mode_shapes.shape[1] // 3
    capacity = max(2, 2 * node_count // devices_slab)
    destination = owner_dev[:, 0]
    onehot_dest = (
        destination[:, None] == jnp.arange(devices_slab, dtype=jnp.int32)[None, :]
    ).astype(jnp.int32)
    ranking = jnp.sum((jnp.cumsum(onehot_dest, axis=0) - 1) * onehot_dest, axis=1)
    slot_of = destination * capacity + ranking
    slot_total = devices_slab * capacity
    cell_tags = (
        jnp.full((slot_total,), -1.0, jnp.float32).at[slot_of].set(owner_cell.astype(jnp.float32))
    )
    contribution = couple(wall_coupling, mode_shapes)
    outgoing = (
        jnp.zeros((slot_total, contribution.shape[1]), jnp.float32).at[slot_of].set(contribution)
    )
    arrived, arrived_tags = (
        lax.all_to_all(outgoing, "slab", split_axis=0, concat_axis=0, tiled=True),
        lax.all_to_all(cell_tags, "slab", split_axis=0, concat_axis=0, tiled=True),
    )
    matches = (
        arrived_tags.astype(jnp.int32)[:, None] == jnp.arange(cell_count, dtype=jnp.int32)[None, :]
    ).astype(jnp.float32)
    forcing = lax.dot_general(
        arrived, matches, (((0,), (0,)), ((), ())), precision=lax.Precision.HIGHEST
    )
    forcing = forcing.reshape(VARS, modes_total, cell_count)
    rim_width = cell_count // 8
    first_cell = lax.axis_index("slab") * cell_count - rim_width
    local_ids = jnp.where(neighbours >= 0, neighbours - first_cell, cell_count + 2 * rim_width)
    state_field = apply_blocks(inv_blocks, forcing)
    for sweep_step in range(SWEEPS):
        widened = with_halo(state_field, (("slab", 2),), rim_width)
        padded = jnp.concatenate(
            [widened, jnp.zeros(widened.shape[:2] + (1,), jnp.float32)], axis=2
        )
        coupled = jnp.zeros_like(state_field)
        for slot_index in range(NBR):
            gathered = jnp.take(padded, local_ids[slot_index], axis=2)
            coupled = coupled + apply_blocks(coupling_blocks[slot_index], gathered)
        state_field = apply_blocks(inv_blocks, forcing - coupled)
    block_width = modes_total // 4
    factor = jnp.zeros((modes_total, modes_total), jnp.float32)
    basis_parts = []
    for block_index in range(4):
        start_col = block_index * block_width
        panel_cols = state_field[:, start_col : start_col + block_width, :]
        if block_index > 0:
            previous = jnp.concatenate(basis_parts, axis=1)
            projection = lax.psum(gram_matrix(previous, panel_cols), "slab")
            panel_cols = panel_cols - combine(projection, previous)
            factor = factor.at[:start_col, start_col : start_col + block_width].set(projection)
        diag_block = cholesky_upper(lax.psum(gram_matrix(panel_cols, panel_cols), "slab"))
        factor = factor.at[
            start_col : start_col + block_width, start_col : start_col + block_width
        ].set(diag_block)
        basis_parts.append(combine(upper_inverse(diag_block), panel_cols))
    basis_out = jnp.concatenate(basis_parts, axis=1)
    norm_scale = math.sqrt(VARS * cell_count * devices_slab)
    return (basis_out * norm_scale, factor / norm_scale)


def solution(mesh):
    in_specs = (
        P(("groups", "slab"), None),
        P(("groups", "slab"), None),
        P(("groups", "slab"), None),
        P(("groups", "slab")),
        P(None, ("groups", "slab")),
        P(None, None, None, ("groups", "slab")),
        P(None, None, ("groups", "slab")),
    )
    out_specs = (P(None, None, ("groups", "slab")), P("groups", None))
    return jax.shard_map(local, mesh=mesh, in_specs=in_specs, out_specs=out_specs, check_vma=False)
```

profile of v0, /device:TPU:0, one launch (start us, length us, event | category | flops | bytes accessed | tf_op | source)
XLA Modules:
  0.0 1054.8 jit_solution(16598022416229044817)
XLA Ops:
  8.1 7.4 all-to-all-start.1
  52.9 27.0 %all-to-all-done = f32[16,64,320]{2,1,0:T(8,128)S(1)} async-done(((f32[16,64,320]{2,1,0:T(8,128)}), f32[16,64,320]{2,1,0:T(8,128)S(1)}, u32[]{:S(2)}, u32[]{:S(2)}) %all-to-all-start) | async-done | bytes 1310752 | tf_op jit(solution)/shard_map/all_to_all | solution.py:113
  98.3 7.6 copy.130
  105.9 19.7 %gather_fusion.5 = f32[2048,5,64]{2,1,0:T(8,128)} fusion(f32[5,64,2561]{1,0,2:T(8,128)} %copy.130, s32[2048]{0:T(1024)} %get-tuple-element.1568), kind=kCustom, calls=%fused_computation.5.clone | custom fusion | bytes 5251072 | tf_op jit(solution)/shard_map/jit(_take)/gather | solution.py:134
  131.7 19.6 %gather_fusion.4 = f32[2048,5,64]{2,1,0:T(8,128)} fusion(f32[5,64,2561]{1,0,2:T(8,128)} %copy.130, s32[2048]{0:T(1024)S(1)} %copy-done.195), kind=kCustom, calls=%fused_computation.4.clone | custom fusion | bytes 5251072 | tf_op jit(solution)/shard_map/jit(_take)/gather | solution.py:134
  157.4 19.6 %gather_fusion.3 = f32[2048,5,64]{2,1,0:T(8,128)} fusion(f32[5,64,2561]{1,0,2:T(8,128)} %copy.130, s32[2048]{0:T(1024)S(1)} %copy-done.193), kind=kCustom, calls=%fused_computation.3.clone | custom fusion | bytes 5251072 | tf_op jit(solution)/shard_map/jit(_take)/gather | solution.py:134
  183.1 19.6 %gather_fusion.2 = f32[2048,5,64]{2,1,0:T(8,128)} fusion(f32[5,64,2561]{1,0,2:T(8,128)} %copy.130, s32[2048]{0:T(1024)S(1)} %copy-done.198), kind=kCustom, calls=%fused_computation.2.clone | custom fusion | bytes 5251072 | tf_op jit(solution)/shard_map/jit(_take)/gather | solution.py:134
  208.8 19.6 %gather_fusion.1 = f32[2048,5,64]{2,1,0:T(8,128)} fusion(f32[5,64,2561]{1,0,2:T(8,128)} %copy.130, s32[2048]{0:T(1024)S(1)} %copy-done.196), kind=kCustom, calls=%fused_computation.1.clone | custom fusion | bytes 5251072 | tf_op jit(solution)/shard_map/jit(_take)/gather | solution.py:134
  234.5 19.6 %gather_fusion = f32[2048,5,64]{2,1,0:T(8,128)} fusion(f32[5,64,2561]{1,0,2:T(8,128)} %copy.130, s32[2048]{0:T(1024)S(1)} %get-tuple-element.1569), kind=kCustom, calls=%fused_computation.clone | custom fusion | bytes 5251072 | tf_op jit(solution)/shard_map/jit(_take)/gather | solution.py:134
  291.8 7.3 collective-permute-start.2
  304.6 7.6 copy.147
  312.3 19.7 %gather_fusion.11 = f32[2048,5,64]{2,1,0:T(8,128)} fusion(f32[5,64,2561]{1,0,2:T(8,128)} %copy.147, s32[2048]{0:T(1024)} %get-tuple-element.1568), kind=kCustom, calls=%fused_computation.11.clone | custom fusion | bytes 5251072 | tf_op jit(solution)/shard_map/jit(_take)/gather | solution.py:134
  332.0 19.8 %gather_fusion.10 = f32[2048,5,64]{2,1,0:T(8,128)} fusion(f32[5,64,2561]{1,0,2:T(8,128)} %copy.147, s32[2048]{0:T(1024)} %get-tuple-element.1567), kind=kCustom, calls=%fused_computation.10.clone | custom fusion | bytes 5251072 | tf_op jit(solution)/shard_map/jit(_take)/gather | solution.py:134
  351.9 19.7 %gather_fusion.9 = f32[2048,5,64]{2,1,0:T(8,128)} fusion(f32[5,64,2561]{1,0,2:T(8,128)} %copy.147, s32[2048]{0:T(1024)S(1)} %copy-done.194), kind=kCustom, calls=%fused_computation.9.clone | custom fusion | bytes 5251072 | tf_op jit(solution)/shard_map/jit(_take)/gather | solution.py:134
  371.5 19.8 %gather_fusion.8 = f32[2048,5,64]{2,1,0:T(8,128)} fusion(f32[5,64,2561]{1,0,2:T(8,128)} %copy.147, s32[2048]{0:T(1024)} %get-tuple-element.1565), kind=kCustom, calls=%fused_computation.8.clone | custom fusion | bytes 5251072 | tf_op jit(solution)/shard_map/jit(_take)/gather | solution.py:134
  391.4 19.8 %gather_fusion.7 = f32[2048,5,64]{2,1,0:T(8,128)} fusion(f32[5,64,2561]{1,0,2:T(8,128)} %copy.147, s32[2048]{0:T(1024)S(1)} %copy-done.197), kind=kCustom, calls=%fused_computation.7.clone | custom fusion | bytes 5251072 | tf_op jit(solution)/shard_map/jit(_take)/gather | solution.py:134
  411.2 19.7 %gather_fusion.6 = f32[2048,5,64]{2,1,0:T(8,128)} fusion(f32[5,64,2561]{1,0,2:T(8,128)} %copy.147, s32[2048]{0:T(1024)} %copy-done.199), kind=kCustom, calls=%fused_computation.6.clone | custom fusion | bytes 5251072 | tf_op jit(solution)/shard_map/jit(_take)/gather | solution.py:134
  511.8 37.7 %psum.49 = f32[16,16]{1,0:T(8,128)S(1)} all-reduce(f32[16,16]{1,0:T(8,128)S(1)} %convolution_bitcast_fusion.20), channel_id=1, replica_groups=mesh['groups'=2,'slab'=16] {'slab'}, use_global_device_ids=true, to_apply=%region_5.7 | all-reduce | flops 256 | bytes 2048 | tf_op jit(solution)/shard_map/psum | solution.py:148
  549.6 24.4 %while.139 = (s32[]{:T(128)}, f32[16,16]{1,0:T(8,128)S(1)}, f32[16,16]{0,1:T(8,128)S(1)}, s32[]{:T(128)}, s32[]{:T(128)}) while((s32[]{:T(128)}, f32[16,16]{1,0:T(8,128)S(1)}, f32[16,16]{0,1:T(8,128)S(1)}, s32[]{:T(128)}, s32[]{:T(128)}) %tuple.552), condition=%wide.region_7.9_spmd.clone.clone, body=%wide.region_6.8_spmd.clone.clone.sunk | while | flops 3955 | bytes 14736 | solution.py:68
  574.0 34.1 %while.140 = (s32[]{:T(128)}, f32[16,16]{1,0:T(8,128)S(1)}, f32[16,16]{1,0:T(8,128)}, f32[16,16]{1,0:T(8,128)S(1)}, s32[]{:T(128)}, /*index=5*/s32[]{:T(128)}, s32[]{:T(128)}) while((s32[]{:T(128)}, f32[16,16]{1,0:T(8,128)S(1)}, f32[16,16]{1,0:T(8,128)}, f32[16,16]{1,0:T(8,128)S(1)}, s32[]{:T(128)}, ...), condition=%wide.region_9.11_spmd.clone.clone, body=%wide.region_8.10_spmd.clone.clone.sunk | while | flops 3924 | bytes 13155 | solution.py:86
  609.8 30.0 %psum.50 = f32[16,16]{1,0:T(8,128)S(1)} all-reduce(f32[16,16]{1,0:T(8,128)S(1)} %convolution_bitcast_fusion.19), channel_id=1, replica_groups=mesh['groups'=2,'slab'=16] {'slab'}, use_global_device_ids=true, to_apply=%region_10.12 | all-reduce | flops 256 | bytes 2048 | tf_op jit(solution)/shard_map/psum | solution.py:145
  642.6 30.0 %psum.51 = f32[16,16]{1,0:T(8,128)S(1)} all-reduce(f32[16,16]{1,0:T(8,128)S(1)} %convolution_bitcast_fusion.18), channel_id=1, replica_groups=mesh['groups'=2,'slab'=16] {'slab'}, use_global_device_ids=true, to_apply=%region_11.13 | all-reduce | flops 256 | bytes 2048 | tf_op jit(solution)/shard_map/psum | solution.py:148
  672.7 24.4 %while.141 = (s32[]{:T(128)}, f32[16,16]{1,0:T(8,128)S(1)}, f32[16,16]{0,1:T(8,128)S(1)}, s32[]{:T(128)}, s32[]{:T(128)}) while((s32[]{:T(128)}, f32[16,16]{1,0:T(8,128)S(1)}, f32[16,16]{0,1:T(8,128)S(1)}, s32[]{:T(128)}, s32[]{:T(128)}) %tuple.551), condition=%wide.region_13.15_spmd.clone.clone, body=%wide.region_12.14_spmd.clone.clone.sunk | while | flops 3955 | bytes 14736 | solution.py:68
  697.1 34.1 %while.142 = (s32[]{:T(128)}, f32[16,16]{1,0:T(8,128)S(1)}, f32[16,16]{1,0:T(8,128)}, f32[16,16]{1,0:T(8,128)S(1)}, s32[]{:T(128)}, /*index=5*/s32[]{:T(128)}, s32[]{:T(128)}) while((s32[]{:T(128)}, f32[16,16]{1,0:T(8,128)S(1)}, f32[16,16]{1,0:T(8,128)}, f32[16,16]{1,0:T(8,128)S(1)}, s32[]{:T(128)}, ...), condition=%wide.region_15.17_spmd.clone.clone, body=%wide.region_14.16_spmd.clone.clone.sunk | while | flops 3924 | bytes 13155 | solution.py:86
  734.2 57.9 %psum.52 = f32[32,16]{1,0:T(8,128)S(1)} all-reduce(f32[32,16]{1,0:T(8,128)S(1)} %convolution_bitcast_fusion.15), channel_id=1, replica_groups=mesh['groups'=2,'slab'=16] {'slab'}, use_global_device_ids=true, to_apply=%region_16.18 | all-reduce | flops 512 | bytes 4096 | tf_op jit(solution)/shard_map/psum | solution.py:145
  803.9 30.0 %psum.53 = f32[16,16]{1,0:T(8,128)S(1)} all-reduce(f32[16,16]{1,0:T(8,128)S(1)} %convolution_bitcast_fusion.17), channel_id=1, replica_groups=mesh['groups'=2,'slab'=16] {'slab'}, use_global_device_ids=true, to_apply=%region_17.19 | all-reduce | flops 256 | bytes 2048 | tf_op jit(solution)/shard_map/psum | solution.py:148
  834.0 24.4 %while.143 = (s32[]{:T(128)}, f32[16,16]{1,0:T(8,128)S(1)}, f32[16,16]{0,1:T(8,128)S(1)}, s32[]{:T(128)}, s32[]{:T(128)}) while((s32[]{:T(128)}, f32[16,16]{1,0:T(8,128)S(1)}, f32[16,16]{0,1:T(8,128)S(1)}, s32[]{:T(128)}, s32[]{:T(128)}) %tuple.550), condition=%wide.region_19.21_spmd.clone.clone, body=%wide.region_18.20_spmd.clone.clone.sunk | while | flops 3955 | bytes 14736 | solution.py:68
  858.4 34.1 %while.144 = (s32[]{:T(128)}, f32[16,16]{1,0:T(8,128)S(1)}, f32[16,16]{1,0:T(8,128)}, f32[16,16]{1,0:T(8,128)S(1)}, s32[]{:T(128)}, /*index=5*/s32[]{:T(128)}, s32[]{:T(128)}) while((s32[]{:T(128)}, f32[16,16]{1,0:T(8,128)S(1)}, f32[16,16]{1,0:T(8,128)}, f32[16,16]{1,0:T(8,128)S(1)}, s32[]{:T(128)}, ...), condition=%wide.region_21.23_spmd.clone.clone, body=%wide.region_20.22_spmd.clone.clone.sunk | while | flops 3924 | bytes 13155 | solution.py:86
  896.0 57.6 %psum.54 = f32[48,16]{1,0:T(8,128)S(1)} all-reduce(f32[48,16]{1,0:T(8,128)S(1)} %fusion.90), channel_id=1, replica_groups=mesh['groups'=2,'slab'=16] {'slab'}, use_global_device_ids=true, to_apply=%region_22.24 | all-reduce | flops 768 | bytes 6144 | tf_op jit(solution)/shard_map/psum | solution.py:145
  962.0 30.0 %psum.55 = f32[16,16]{1,0:T(8,128)S(1)} all-reduce(f32[16,16]{1,0:T(8,128)S(1)} %convolution_bitcast_fusion.16), channel_id=1, replica_groups=mesh['groups'=2,'slab'=16] {'slab'}, use_global_device_ids=true, to_apply=%region_23.25 | all-reduce | flops 256 | bytes 2048 | tf_op jit(solution)/shard_map/psum | solution.py:148
  992.1 24.4 %while.145 = (s32[]{:T(128)}, f32[16,16]{1,0:T(8,128)S(1)}, f32[16,16]{0,1:T(8,128)S(1)}, s32[]{:T(128)}, s32[]{:T(128)}) while((s32[]{:T(128)}, f32[16,16]{1,0:T(8,128)S(1)}, f32[16,16]{0,1:T(8,128)S(1)}, s32[]{:T(128)}, s32[]{:T(128)}) %tuple.549), condition=%wide.region_25.27_spmd.clone.clone, body=%wide.region_24.26_spmd.clone.clone.sunk | while | flops 3955 | bytes 14736 | solution.py:68
  1016.6 34.1 %while.146 = (s32[]{:T(128)}, f32[16,16]{1,0:T(8,128)S(1)}, f32[16,16]{1,0:T(8,128)}, f32[16,16]{1,0:T(8,128)S(1)}, s32[]{:T(128)}, /*index=5*/s32[]{:T(128)}, s32[]{:T(128)}) while((s32[]{:T(128)}, f32[16,16]{1,0:T(8,128)S(1)}, f32[16,16]{1,0:T(8,128)}, f32[16,16]{1,0:T(8,128)S(1)}, s32[]{:T(128)}, ...), condition=%wide.region_27.29_spmd.clone.clone, body=%wide.region_26.28_spmd.clone.clone.sunk | while | flops 3924 | bytes 13155 | solution.py:86
  (1295 shorter events, 438.7 us)
Async XLA Ops:
  8.1 33.1 %all-to-all-start.1 = ((f32[16,64,1]{1,2,0:T(1,128)}), f32[16,64,1]{1,2,0:T(1,128)S(1)}, u32[]{:S(2)}, u32[]{:S(2)}) async-start(f32[16,64,1]{1,2,0:T(1,128)} %bitcast.16), calls=%async_computation.1 | async-start | bytes 16384 | tf_op jit(solution)/shard_map/all_to_all | solution.py:114
  41.8 38.2 %all-to-all-start = ((f32[16,64,320]{2,1,0:T(8,128)}), f32[16,64,320]{2,1,0:T(8,128)S(1)}, u32[]{:S(2)}, u32[]{:S(2)}) async-start(f32[16,64,320]{2,1,0:T(8,128)} %bitcast.14), calls=%async_computation | async-start | bytes 3145728 | tf_op jit(solution)/shard_map/all_to_all | solution.py:113
  51.6 223.7 %copy-start.129 = (f32[1,1,2048]{2,1,0:T(1,128)}, f32[1,1,2048]{2,1,0:T(1,128)S(1)}, u32[]{:S(2)}) copy-start(f32[1,1,2048]{2,1,0:T(1,128)S(1)} %get-tuple-element.1472) | copy-start | bytes 24580
  51.8 224.3 %copy-start.121 = (f32[1,1,2048]{2,1,0:T(1,128)}, f32[1,1,2048]{2,1,0:T(1,128)S(1)}, u32[]{:S(2)}) copy-start(f32[1,1,2048]{2,1,0:T(1,128)S(1)} %get-tuple-element.1462) | copy-start | bytes 24580
  51.8 224.3 %copy-start.123 = (f32[1,1,2048]{2,1,0:T(1,128)}, f32[1,1,2048]{2,1,0:T(1,128)S(1)}, u32[]{:S(2)}) copy-start(f32[1,1,2048]{2,1,0:T(1,128)S(1)} %get-tuple-element.1463) | copy-start | bytes 24580
  51.8 224.3 %copy-start.125 = (f32[1,1,2048]{2,1,0:T(1,128)}, f32[1,1,2048]{2,1,0:T(1,128)S(1)}, u32[]{:S(2)}) copy-start(f32[1,1,2048]{2,1,0:T(1,128)S(1)} %get-tuple-element.1464) | copy-start | bytes 24580
  51.8 224.3 %copy-start.127 = (f32[1,1,2048]{2,1,0:T(1,128)}, f32[1,1,2048]{2,1,0:T(1,128)S(1)}, u32[]{:S(2)}) copy-start(f32[1,1,2048]{2,1,0:T(1,128)S(1)} %get-tuple-element.1465) | copy-start | bytes 24580
  51.8 224.5 %copy-start.111 = (f32[1,1,2048]{2,1,0:T(1,128)}, f32[1,1,2048]{2,1,0:T(1,128)S(1)}, u32[]{:S(2)}) copy-start(f32[1,1,2048]{2,1,0:T(1,128)S(1)} %get-tuple-element.1457) | copy-start | bytes 24580
  51.8 224.5 %copy-start.113 = (f32[1,1,2048]{2,1,0:T(1,128)}, f32[1,1,2048]{2,1,0:T(1,128)S(1)}, u32[]{:S(2)}) copy-start(f32[1,1,2048]{2,1,0:T(1,128)S(1)} %get-tuple-element.1458) | copy-start | bytes 24580
  51.8 224.5 %copy-start.115 = (f32[1,1,2048]{2,1,0:T(1,128)}, f32[1,1,2048]{2,1,0:T(1,128)S(1)}, u32[]{:S(2)}) copy-start(f32[1,1,2048]{2,1,0:T(1,128)S(1)} %get-tuple-element.1459) | copy-start | bytes 24580
  51.8 224.5 %copy-start.117 = (f32[1,1,2048]{2,1,0:T(1,128)}, f32[1,1,2048]{2,1,0:T(1,128)S(1)}, u32[]{:S(2)}) copy-start(f32[1,1,2048]{2,1,0:T(1,128)S(1)} %get-tuple-element.1460) | copy-start | bytes 24580
  51.8 224.5 %copy-start.119 = (f32[1,1,2048]{2,1,0:T(1,128)}, f32[1,1,2048]{2,1,0:T(1,128)S(1)}, u32[]{:S(2)}) copy-start(f32[1,1,2048]{2,1,0:T(1,128)S(1)} %get-tuple-element.1461) | copy-start | bytes 24580
  51.9 224.7 %copy-start.101 = (f32[1,1,2048]{2,1,0:T(1,128)}, f32[1,1,2048]{2,1,0:T(1,128)S(1)}, u32[]{:S(2)}) copy-start(f32[1,1,2048]{2,1,0:T(1,128)S(1)} %get-tuple-element.1452) | copy-start | bytes 24580
  51.9 224.7 %copy-start.103 = (f32[1,1,2048]{2,1,0:T(1,128)}, f32[1,1,2048]{2,1,0:T(1,128)S(1)}, u32[]{:S(2)}) copy-start(f32[1,1,2048]{2,1,0:T(1,128)S(1)} %get-tuple-element.1453) | copy-start | bytes 24580
  51.9 224.7 %copy-start.105 = (f32[1,1,2048]{2,1,0:T(1,128)}, f32[1,1,2048]{2,1,0:T(1,128)S(1)}, u32[]{:S(2)}) copy-start(f32[1,1,2048]{2,1,0:T(1,128)S(1)} %get-tuple-element.1454) | copy-start | bytes 24580
  51.9 224.7 %copy-start.107 = (f32[1,1,2048]{2,1,0:T(1,128)}, f32[1,1,2048]{2,1,0:T(1,128)S(1)}, u32[]{:S(2)}) copy-start(f32[1,1,2048]{2,1,0:T(1,128)S(1)} %get-tuple-element.1455) | copy-start | bytes 24580
  51.9 224.7 %copy-start.109 = (f32[1,1,2048]{2,1,0:T(1,128)}, f32[1,1,2048]{2,1,0:T(1,128)S(1)}, u32[]{:S(2)}) copy-start(f32[1,1,2048]{2,1,0:T(1,128)S(1)} %get-tuple-element.1456) | copy-start | bytes 24580
  51.9 225.0 %copy-start.91 = (f32[1,1,2048]{2,1,0:T(1,128)}, f32[1,1,2048]{2,1,0:T(1,128)S(1)}, u32[]{:S(2)}) copy-start(f32[1,1,2048]{2,1,0:T(1,128)S(1)} %get-tuple-element.1447) | copy-start | bytes 24580
  51.9 225.0 %copy-start.93 = (f32[1,1,2048]{2,1,0:T(1,128)}, f32[1,1,2048]{2,1,0:T(1,128)S(1)}, u32[]{:S(2)}) copy-start(f32[1,1,2048]{2,1,0:T(1,128)S(1)} %get-tuple-element.1448) | copy-start | bytes 24580
  51.9 225.0 %copy-start.95 = (f32[1,1,2048]{2,1,0:T(1,128)}, f32[1,1,2048]{2,1,0:T(1,128)S(1)}, u32[]{:S(2)}) copy-start(f32[1,1,2048]{2,1,0:T(1,128)S(1)} %get-tuple-element.1449) | copy-start | bytes 24580
  51.9 225.0 %copy-start.97 = (f32[1,1,2048]{2,1,0:T(1,128)}, f32[1,1,2048]{2,1,0:T(1,128)S(1)}, u32[]{:S(2)}) copy-start(f32[1,1,2048]{2,1,0:T(1,128)S(1)} %get-tuple-element.1450) | copy-start | bytes 24580
  51.9 225.0 %copy-start.99 = (f32[1,1,2048]{2,1,0:T(1,128)}, f32[1,1,2048]{2,1,0:T(1,128)S(1)}, u32[]{:S(2)}) copy-start(f32[1,1,2048]{2,1,0:T(1,128)S(1)} %get-tuple-element.1451) | copy-start | bytes 24580
  52.1 225.5 %copy-start.83 = (f32[1,1,2048]{2,1,0:T(1,128)}, f32[1,1,2048]{2,1,0:T(1,128)S(1)}, u32[]{:S(2)}) copy-start(f32[1,1,2048]{2,1,0:T(1,128)S(1)} %get-tuple-element.1437) | copy-start | bytes 24580
  52.1 225.5 %copy-start.85 = (f32[1,1,2048]{2,1,0:T(1,128)}, f32[1,1,2048]{2,1,0:T(1,128)S(1)}, u32[]{:S(2)}) copy-start(f32[1,1,2048]{2,1,0:T(1,128)S(1)} %get-tuple-element.1438) | copy-start | bytes 24580
  52.1 225.5 %copy-start.87 = (f32[1,1,2048]{2,1,0:T(1,128)}, f32[1,1,2048]{2,1,0:T(1,128)S(1)}, u32[]{:S(2)}) copy-start(f32[1,1,2048]{2,1,0:T(1,128)S(1)} %get-tuple-element.1439) | copy-start | bytes 24580
  52.1 225.5 %copy-start.89 = (f32[1,1,2048]{2,1,0:T(1,128)}, f32[1,1,2048]{2,1,0:T(1,128)S(1)}, u32[]{:S(2)}) copy-start(f32[1,1,2048]{2,1,0:T(1,128)S(1)} %get-tuple-element.1440) | copy-start | bytes 24580
  52.1 225.8 %copy-start.79 = (f32[1,1,2048]{2,1,0:T(1,128)}, f32[1,1,2048]{2,1,0:T(1,128)S(1)}, u32[]{:S(2)}) copy-start(f32[1,1,2048]{2,1,0:T(1,128)S(1)} %get-tuple-element.1435) | copy-start | bytes 24580
  52.1 225.8 %copy-start.81 = (f32[1,1,2048]{2,1,0:T(1,128)}, f32[1,1,2048]{2,1,0:T(1,128)S(1)}, u32[]{:S(2)}) copy-start(f32[1,1,2048]{2,1,0:T(1,128)S(1)} %get-tuple-element.1436) | copy-start | bytes 24580
  88.5 5.1 collective-permute-start
  91.2 5.0 collective-permute-start.1
  291.8 10.5 collective-permute-start.2
  299.1 3.5 collective-permute-start.3
  (193 other events, 4023.8 us)
where the time goes:
time: 1070 us; the launch traced here: 1050 us
  local copies, waits for them, and re-layouts  451 us (42%)
  blocking collectives  273 us (26%)
  matrix products  127 us (12%)
  other arithmetic  98.8 us (9%)
  loops' own time  45.6 us (4%)
  waiting for transfers between devices  30 us (3%)
  starting transfers between devices  26.2 us (2%)
    gather x24, local copies, waits for them, and re-layouts, local(): gathered = jnp.take(padded, local_ids[slot_index], axis=2)  310 us
    psum x3, blocking collectives, local(): projection = lax.psum(gram_matrix(previous, panel_cols), 'slab')  146 us
    psum x4, blocking collectives, local(): lax.psum(gram_matrix(panel_cols, panel_cols), 'slab')  128 us
    dot_general x64, matrix products, row_step(): jnp.dot(earlier, inverse, precision=lax.Precision.HIGHEST)  93.2 us
    another operation x4, loops' own time, cholesky_upper(): lax.fori_loop(0, order, column_step, jnp.zeros((order, order), jnp.float32))  45.1 us
    dynamic_slice x64, local copies, waits for them, and re-layouts, column_step(): lax.dynamic_index_in_dim(reduced, column_at, 0, keepdims=False)  38 us
    dynamic_slice x64, local copies, waits for them, and re-layouts, row_step(): pivot = lax.dynamic_index_in_dim(lower_row, row_at, 0, keepdims=False)  37.7 us
    unnamed x68, other arithmetic  29.4 us
  transfers between devices with their start and end apart: 6, of which 3 were waited for; matrix products, arithmetic and copies ran while one was open for 3% of the time, Pallas kernels for 0%

commit v1 on v0

--- a/solution.py
+++ b/solution.py
@@ -7,6 +7,18 @@
 VARS = 5
 NBR = 6
 SWEEPS = 2
+
+
+def exchange_directly(value, axis, split, join):
+    ways, here = (lax.axis_size(axis), lax.axis_index(axis))
+    width = value.shape[split] // ways
+    turned = jnp.roll(value, -here * width, axis=split)
+    got = [lax.slice_in_dim(turned, 0, width, axis=split)]
+    for far in range(1, ways):
+        sent = lax.slice_in_dim(turned, far * width, (far + 1) * width, axis=split)
+        got.append(lax.ppermute(sent, axis, [(d, (d + far) % ways) for d in range(ways)]))
+    line = jnp.concatenate(got[::-1], axis=join)
+    return jnp.roll(line, (here + 1) * got[0].shape[join], axis=join)
 
 
 def with_halo(x, sides, width):
@@ -110,7 +122,7 @@
         jnp.zeros((slot_total, contribution.shape[1]), jnp.float32).at[slot_of].set(contribution)
     )
     arrived, arrived_tags = (
-        lax.all_to_all(outgoing, "slab", split_axis=0, concat_axis=0, tiled=True),
+        exchange_directly(outgoing, "slab", 0, 0),
         lax.all_to_all(cell_tags, "slab", split_axis=0, concat_axis=0, tiled=True),
     )
     matches = (

time: 1070 us -> 1100 us (1.028)
  starting transfers between devices: 26.2 us -> 59.4 us
    ppermute x0 -> x15, starting transfers between devices: none -> 36.4 us  [exchange_directly(): lax.ppermute(sent, axis, [(d, (d + far) % ways) for d in range(ways)])]
    ppermute x0 -> x15, waiting for transfers between devices: none -> 29.5 us  [exchange_directly(): lax.ppermute(sent, axis, [(d, (d + far) % ways) for d in range(ways)])]
    all_to_all x1 -> x0, waiting for transfers between devices: 27 us -> none  [local(): lax.all_to_all(outgoing, 'slab', split_axis=0, concat_axis=0, tiled=True)]
  transfers between devices with their start and end apart: 6 -> 20, of which waited for: 3 -> 12; matrix products, arithmetic and copies ran while one was open for 3% -> 3% of each run, Pallas kernels for 0% -> 0%
where the time goes in v1:
time: 1100 us; the launch traced here: 1090 us
  local copies, waits for them, and re-layouts  456 us (41%)
  blocking collectives  271 us (25%)
  matrix products  125 us (11%)
  other arithmetic  94.5 us (9%)
  starting transfers between devices  59.4 us (5%)
  loops' own time  45.6 us (4%)
  waiting for transfers between devices  35.8 us (3%)
    gather x24, local copies, waits for them, and re-layouts, local(): gathered = jnp.take(padded, local_ids[slot_index], axis=2)  310 us
    psum x3, blocking collectives, local(): projection = lax.psum(gram_matrix(previous, panel_cols), 'slab')  146 us
    psum x4, blocking collectives, local(): lax.psum(gram_matrix(panel_cols, panel_cols), 'slab')  125 us
    dot_general x64, matrix products, row_step(): jnp.dot(earlier, inverse, precision=lax.Precision.HIGHEST)  92.2 us
    another operation x4, loops' own time, cholesky_upper(): lax.fori_loop(0, order, column_step, jnp.zeros((order, order), jnp.float32))  45.1 us
    dynamic_slice x64, local copies, waits for them, and re-layouts, column_step(): lax.dynamic_index_in_dim(reduced, column_at, 0, keepdims=False)  38 us
    dynamic_slice x64, local copies, waits for them, and re-layouts, row_step(): pivot = lax.dynamic_index_in_dim(lower_row, row_at, 0, keepdims=False)  37.7 us
    ppermute x15, starting transfers between devices, exchange_directly(): lax.ppermute(sent, axis, [(d, (d + far) % ways) for d in range(ways)])  36.4 us
  transfers between devices with their start and end apart: 20, of which 12 were waited for; matrix products, arithmetic and copies ran while one was open for 3% of the time, Pallas kernels for 0%

profile of v1, /device:TPU:0, one launch (start us, length us, event | category | flops | bytes accessed | tf_op | source)
XLA Modules:
  0.0 1089.8 jit_solution(13711698549814982445)
XLA Ops:
  8.0 7.4 all-to-all-start
  136.8 7.7 copy.130
  144.5 19.7 %gather_fusion.5 = f32[2048,5,64]{2,1,0:T(8,128)} fusion(f32[5,64,2561]{1,0,2:T(8,128)} %copy.130, s32[2048]{0:T(1024)S(1)} %get-tuple-element.1584), kind=kCustom, calls=%fused_computation.5.clone | custom fusion | bytes 5251072 | tf_op jit(solution)/shard_map/jit(_take)/gather | solution.py:146
  170.2 19.7 %gather_fusion.4 = f32[2048,5,64]{2,1,0:T(8,128)} fusion(f32[5,64,2561]{1,0,2:T(8,128)} %copy.130, s32[2048]{0:T(1024)S(1)} %copy-done.224), kind=kCustom, calls=%fused_computation.4.clone | custom fusion | bytes 5251072 | tf_op jit(solution)/shard_map/jit(_take)/gather | solution.py:146
  196.1 19.7 %gather_fusion.3 = f32[2048,5,64]{2,1,0:T(8,128)} fusion(f32[5,64,2561]{1,0,2:T(8,128)} %copy.130, s32[2048]{0:T(1024)S(1)} %copy-done.222), kind=kCustom, calls=%fused_computation.3.clone | custom fusion | bytes 5251072 | tf_op jit(solution)/shard_map/jit(_take)/gather | solution.py:146
  221.9 19.7 %gather_fusion.2 = f32[2048,5,64]{2,1,0:T(8,128)} fusion(f32[5,64,2561]{1,0,2:T(8,128)} %copy.130, s32[2048]{0:T(1024)S(1)} %copy-done.227), kind=kCustom, calls=%fused_computation.2.clone | custom fusion | bytes 5251072 | tf_op jit(solution)/shard_map/jit(_take)/gather | solution.py:146
  247.6 19.7 %gather_fusion.1 = f32[2048,5,64]{2,1,0:T(8,128)} fusion(f32[5,64,2561]{1,0,2:T(8,128)} %copy.130, s32[2048]{0:T(1024)S(1)} %copy-done.225), kind=kCustom, calls=%fused_computation.1.clone | custom fusion | bytes 5251072 | tf_op jit(solution)/shard_map/jit(_take)/gather | solution.py:146
  273.4 19.7 %gather_fusion = f32[2048,5,64]{2,1,0:T(8,128)} fusion(f32[5,64,2561]{1,0,2:T(8,128)} %copy.130, s32[2048]{0:T(1024)S(1)} %get-tuple-element.1585), kind=kCustom, calls=%fused_computation.clone | custom fusion | bytes 5251072 | tf_op jit(solution)/shard_map/jit(_take)/gather | solution.py:146
  293.1 6.4 copy.131
  330.4 7.3 collective-permute-start.17
  344.3 7.7 copy.147
  352.0 19.8 %gather_fusion.11 = f32[2048,5,64]{2,1,0:T(8,128)} fusion(f32[5,64,2561]{1,0,2:T(8,128)} %copy.147, s32[2048]{0:T(1024)S(1)} %copy-done.230), kind=kCustom, calls=%fused_computation.11.clone | custom fusion | bytes 5251072 | tf_op jit(solution)/shard_map/jit(_take)/gather | solution.py:146
  371.7 19.9 %gather_fusion.10 = f32[2048,5,64]{2,1,0:T(8,128)} fusion(f32[5,64,2561]{1,0,2:T(8,128)} %copy.147, s32[2048]{0:T(1024)} %get-tuple-element.1583), kind=kCustom, calls=%fused_computation.10.clone | custom fusion | bytes 5251072 | tf_op jit(solution)/shard_map/jit(_take)/gather | solution.py:146
  391.6 19.8 %gather_fusion.9 = f32[2048,5,64]{2,1,0:T(8,128)} fusion(f32[5,64,2561]{1,0,2:T(8,128)} %copy.147, s32[2048]{0:T(1024)S(1)} %copy-done.223), kind=kCustom, calls=%fused_computation.9.clone | custom fusion | bytes 5251072 | tf_op jit(solution)/shard_map/jit(_take)/gather | solution.py:146
  411.4 19.9 %gather_fusion.8 = f32[2048,5,64]{2,1,0:T(8,128)} fusion(f32[5,64,2561]{1,0,2:T(8,128)} %copy.147, s32[2048]{0:T(1024)} %get-tuple-element.1581), kind=kCustom, calls=%fused_computation.8.clone | custom fusion | bytes 5251072 | tf_op jit(solution)/shard_map/jit(_take)/gather | solution.py:146
  431.3 19.8 %gather_fusion.7 = f32[2048,5,64]{2,1,0:T(8,128)} fusion(f32[5,64,2561]{1,0,2:T(8,128)} %copy.147, s32[2048]{0:T(1024)S(1)} %copy-done.226), kind=kCustom, calls=%fused_computation.7.clone | custom fusion | bytes 5251072 | tf_op jit(solution)/shard_map/jit(_take)/gather | solution.py:146
  451.1 19.8 %gather_fusion.6 = f32[2048,5,64]{2,1,0:T(8,128)} fusion(f32[5,64,2561]{1,0,2:T(8,128)} %copy.147, s32[2048]{0:T(1024)} %copy-done.228), kind=kCustom, calls=%fused_computation.6.clone | custom fusion | bytes 5251072 | tf_op jit(solution)/shard_map/jit(_take)/gather | solution.py:146
  550.4 35.4 %psum.49 = f32[16,16]{1,0:T(8,128)S(1)} all-reduce(f32[16,16]{1,0:T(8,128)S(1)} %convolution_bitcast_fusion.20), channel_id=1, replica_groups=mesh['groups'=2,'slab'=16] {'slab'}, use_global_device_ids=true, to_apply=%region_5.8 | all-reduce | flops 256 | bytes 2048 | tf_op jit(solution)/shard_map/psum | solution.py:160
  585.8 24.4 %while.139 = (s32[]{:T(128)}, f32[16,16]{1,0:T(8,128)S(1)}, f32[16,16]{0,1:T(8,128)S(1)}, s32[]{:T(128)}, s32[]{:T(128)}) while((s32[]{:T(128)}, f32[16,16]{1,0:T(8,128)S(1)}, f32[16,16]{0,1:T(8,128)S(1)}, s32[]{:T(128)}, s32[]{:T(128)}) %tuple.567), condition=%wide.region_7.10_spmd.clone.clone, body=%wide.region_6.9_spmd.clone.clone.sunk | while | flops 3955 | bytes 14736 | solution.py:80
  610.3 33.9 %while.140 = (s32[]{:T(128)}, f32[16,16]{1,0:T(8,128)S(1)}, f32[16,16]{1,0:T(8,128)}, f32[16,16]{1,0:T(8,128)S(1)}, s32[]{:T(128)}, /*index=5*/s32[]{:T(128)}, s32[]{:T(128)}) while((s32[]{:T(128)}, f32[16,16]{1,0:T(8,128)S(1)}, f32[16,16]{1,0:T(8,128)}, f32[16,16]{1,0:T(8,128)S(1)}, s32[]{:T(128)}, ...), condition=%wide.region_9.12_spmd.clone.clone, body=%wide.region_8.11_spmd.clone.clone.sunk | while | flops 3924 | bytes 13155 | solution.py:98
  645.8 30.0 %psum.50 = f32[16,16]{1,0:T(8,128)S(1)} all-reduce(f32[16,16]{1,0:T(8,128)S(1)} %convolution_bitcast_fusion.19), channel_id=1, replica_groups=mesh['groups'=2,'slab'=16] {'slab'}, use_global_device_ids=true, to_apply=%region_10.13 | all-reduce | flops 256 | bytes 2048 | tf_op jit(solution)/shard_map/psum | solution.py:157
  678.5 30.0 %psum.51 = f32[16,16]{1,0:T(8,128)S(1)} all-reduce(f32[16,16]{1,0:T(8,128)S(1)} %convolution_bitcast_fusion.18), channel_id=1, replica_groups=mesh['groups'=2,'slab'=16] {'slab'}, use_global_device_ids=true, to_apply=%region_11.14 | all-reduce | flops 256 | bytes 2048 | tf_op jit(solution)/shard_map/psum | solution.py:160
  708.6 24.4 %while.141 = (s32[]{:T(128)}, f32[16,16]{1,0:T(8,128)S(1)}, f32[16,16]{0,1:T(8,128)S(1)}, s32[]{:T(128)}, s32[]{:T(128)}) while((s32[]{:T(128)}, f32[16,16]{1,0:T(8,128)S(1)}, f32[16,16]{0,1:T(8,128)S(1)}, s32[]{:T(128)}, s32[]{:T(128)}) %tuple.566), condition=%wide.region_13.16_spmd.clone.clone, body=%wide.region_12.15_spmd.clone.clone.sunk | while | flops 3955 | bytes 14736 | solution.py:80
  733.0 33.9 %while.142 = (s32[]{:T(128)}, f32[16,16]{1,0:T(8,128)S(1)}, f32[16,16]{1,0:T(8,128)}, f32[16,16]{1,0:T(8,128)S(1)}, s32[]{:T(128)}, /*index=5*/s32[]{:T(128)}, s32[]{:T(128)}) while((s32[]{:T(128)}, f32[16,16]{1,0:T(8,128)S(1)}, f32[16,16]{1,0:T(8,128)}, f32[16,16]{1,0:T(8,128)S(1)}, s32[]{:T(128)}, ...), condition=%wide.region_15.18_spmd.clone.clone, body=%wide.region_14.17_spmd.clone.clone.sunk | while | flops 3924 | bytes 13155 | solution.py:98
  769.9 57.9 %psum.52 = f32[32,16]{1,0:T(8,128)S(1)} all-reduce(f32[32,16]{1,0:T(8,128)S(1)} %convolution_bitcast_fusion.15), channel_id=1, replica_groups=mesh['groups'=2,'slab'=16] {'slab'}, use_global_device_ids=true, to_apply=%region_16.19 | all-reduce | flops 512 | bytes 4096 | tf_op jit(solution)/shard_map/psum | solution.py:157
  839.4 30.0 %psum.53 = f32[16,16]{1,0:T(8,128)S(1)} all-reduce(f32[16,16]{1,0:T(8,128)S(1)} %convolution_bitcast_fusion.17), channel_id=1, replica_groups=mesh['groups'=2,'slab'=16] {'slab'}, use_global_device_ids=true, to_apply=%region_17.20 | all-reduce | flops 256 | bytes 2048 | tf_op jit(solution)/shard_map/psum | solution.py:160
  869.5 24.4 %while.143 = (s32[]{:T(128)}, f32[16,16]{1,0:T(8,128)S(1)}, f32[16,16]{0,1:T(8,128)S(1)}, s32[]{:T(128)}, s32[]{:T(128)}) while((s32[]{:T(128)}, f32[16,16]{1,0:T(8,128)S(1)}, f32[16,16]{0,1:T(8,128)S(1)}, s32[]{:T(128)}, s32[]{:T(128)}) %tuple.565), condition=%wide.region_19.22_spmd.clone.clone, body=%wide.region_18.21_spmd.clone.clone.sunk | while | flops 3955 | bytes 14736 | solution.py:80
  893.9 33.9 %while.144 = (s32[]{:T(128)}, f32[16,16]{1,0:T(8,128)S(1)}, f32[16,16]{1,0:T(8,128)}, f32[16,16]{1,0:T(8,128)S(1)}, s32[]{:T(128)}, /*index=5*/s32[]{:T(128)}, s32[]{:T(128)}) while((s32[]{:T(128)}, f32[16,16]{1,0:T(8,128)S(1)}, f32[16,16]{1,0:T(8,128)}, f32[16,16]{1,0:T(8,128)S(1)}, s32[]{:T(128)}, ...), condition=%wide.region_21.24_spmd.clone.clone, body=%wide.region_20.23_spmd.clone.clone.sunk | while | flops 3924 | bytes 13155 | solution.py:98
  931.3 57.6 %psum.54 = f32[48,16]{1,0:T(8,128)S(1)} all-reduce(f32[48,16]{1,0:T(8,128)S(1)} %fusion.93), channel_id=1, replica_groups=mesh['groups'=2,'slab'=16] {'slab'}, use_global_device_ids=true, to_apply=%region_22.25 | all-reduce | flops 768 | bytes 6144 | tf_op jit(solution)/shard_map/psum | solution.py:157
  997.3 30.0 %psum.55 = f32[16,16]{1,0:T(8,128)S(1)} all-reduce(f32[16,16]{1,0:T(8,128)S(1)} %convolution_bitcast_fusion.16), channel_id=1, replica_groups=mesh['groups'=2,'slab'=16] {'slab'}, use_global_device_ids=true, to_apply=%region_23.26 | all-reduce | flops 256 | bytes 2048 | tf_op jit(solution)/shard_map/psum | solution.py:160
  1027.4 24.4 %while.145 = (s32[]{:T(128)}, f32[16,16]{1,0:T(8,128)S(1)}, f32[16,16]{0,1:T(8,128)S(1)}, s32[]{:T(128)}, s32[]{:T(128)}) while((s32[]{:T(128)}, f32[16,16]{1,0:T(8,128)S(1)}, f32[16,16]{0,1:T(8,128)S(1)}, s32[]{:T(128)}, s32[]{:T(128)}) %tuple.564), condition=%wide.region_25.28_spmd.clone.clone, body=%wide.region_24.27_spmd.clone.clone.sunk | while | flops 3955 | bytes 14736 | solution.py:80
  1051.8 33.9 %while.146 = (s32[]{:T(128)}, f32[16,16]{1,0:T(8,128)S(1)}, f32[16,16]{1,0:T(8,128)}, f32[16,16]{1,0:T(8,128)S(1)}, s32[]{:T(128)}, /*index=5*/s32[]{:T(128)}, s32[]{:T(128)}) while((s32[]{:T(128)}, f32[16,16]{1,0:T(8,128)S(1)}, f32[16,16]{1,0:T(8,128)}, f32[16,16]{1,0:T(8,128)S(1)}, s32[]{:T(128)}, ...), condition=%wide.region_27.30_spmd.clone.clone, body=%wide.region_26.29_spmd.clone.clone.sunk | while | flops 3924 | bytes 13155 | solution.py:98
  (1403 shorter events, 496.1 us)
Async XLA Ops:
  8.0 43.7 %all-to-all-start = ((f32[16,64,1]{1,2,0:T(1,128)}), f32[16,64,1]{1,2,0:T(1,128)}, u32[]{:S(2)}, u32[]{:S(2)}) async-start(f32[16,64,1]{1,2,0:T(1,128)} %bitcast.14), calls=%async_computation | async-start | bytes 16384 | tf_op jit(solution)/shard_map/all_to_all | solution.py:126
  21.9 93.2 %collective-permute-start.14 = (f32[64,320]{1,0:T(8,128)S(1)}, f32[64,320]{1,0:T(8,128)}, u32[]{:S(2)}, u32[]{:S(2)}) collective-permute-start(f32[64,320]{1,0:T(8,128)S(1)} %get-tuple-element.1370), channel_id=1, source_target_pairs={{0,1},{1,2},{2,3},{3,4},{4,5},{5,6},{6,7},{7,8},{8,9},{9,10},{10,1... | collective-permute-start | bytes 245768 | tf_op jit(solution)/shard_map/ppermute | solution.py:19
  22.3 92.0 %collective-permute-start.13 = (f32[64,320]{1,0:T(8,128)S(1)}, f32[64,320]{1,0:T(8,128)}, u32[]{:S(2)}, u32[]{:S(2)}) collective-permute-start(f32[64,320]{1,0:T(8,128)S(1)} %get-tuple-element.1371), channel_id=1, source_target_pairs={{0,2},{1,3},{2,4},{3,5},{4,6},{5,7},{6,8},{7,9},{8,10},{9,11},{10,... | collective-permute-start | bytes 245768 | tf_op jit(solution)/shard_map/ppermute | solution.py:19
  23.9 89.4 %collective-permute-start.12 = (f32[64,320]{1,0:T(8,128)S(1)}, f32[64,320]{1,0:T(8,128)}, u32[]{:S(2)}, u32[]{:S(2)}) collective-permute-start(f32[64,320]{1,0:T(8,128)S(1)} %get-tuple-element.1372), channel_id=1, source_target_pairs={{0,3},{1,4},{2,5},{3,6},{4,7},{5,8},{6,9},{7,10},{8,11},{9,12},{10... | collective-permute-start | bytes 245768 | tf_op jit(solution)/shard_map/ppermute | solution.py:19
  26.2 86.3 %collective-permute-start.11 = (f32[64,320]{1,0:T(8,128)S(1)}, f32[64,320]{1,0:T(8,128)}, u32[]{:S(2)}, u32[]{:S(2)}) collective-permute-start(f32[64,320]{1,0:T(8,128)S(1)} %get-tuple-element.1373), channel_id=1, source_target_pairs={{0,4},{1,5},{2,6},{3,7},{4,8},{5,9},{6,10},{7,11},{8,12},{9,13},{1... | collective-permute-start | bytes 245768 | tf_op jit(solution)/shard_map/ppermute | solution.py:19
  27.6 25.5 %collective-permute-start = (f32[64,320]{1,0:T(8,128)}, f32[64,320]{1,0:T(8,128)}, u32[]{:S(2)}, u32[]{:S(2)}) collective-permute-start(f32[64,320]{1,0:T(8,128)} %get-tuple-element.1384), channel_id=1, source_target_pairs={{0,15},{1,0},{2,1},{3,2},{4,3},{5,4},{6,5},{7,6},{8,7},{9,8},{10,9... | collective-permute-start | bytes 245768 | tf_op jit(solution)/shard_map/ppermute | solution.py:19
  29.6 20.2 %copy-start.233 = (s32[1,2048]{1,0:T(1,128)}, s32[1,2048]{1,0:T(1,128)S(1)}, u32[]{:S(2)}) copy-start(s32[1,2048]{1,0:T(1,128)S(1)} %get-tuple-element.1568) | copy-start | bytes 24580
  53.1 63.0 %copy-start.246 = (s32[1024]{0:T(1024)S(1)}, s32[1024]{0:T(1024)}, u32[]{:S(2)}) copy-start(s32[1024]{0:T(1024)} %convert_element_type.34) | copy-start | bytes 12292
  53.1 4.7 collective-permute-start.1
  57.8 4.0 collective-permute-start.2
  61.8 5.0 collective-permute-start.3
  66.8 6.2 collective-permute-start.4
  73.0 6.3 collective-permute-start.5
  79.3 5.7 collective-permute-start.6
  85.1 7.0 collective-permute-start.7
  92.1 5.8 collective-permute-start.8
  97.9 8.5 collective-permute-start.9
  106.4 6.0 collective-permute-start.10
  122.6 7.5 collective-permute-start.15
  128.2 6.7 collective-permute-start.16
  130.0 143.4 %copy-start.228 = (s32[2048]{0:T(1024)}, s32[2048]{0:T(1024)S(1)}, u32[]{:S(2)}) copy-start(s32[2048]{0:T(1024)S(1)} %get-tuple-element.1585) | copy-start | bytes 24580
  330.4 10.4 collective-permute-start.17
  337.7 4.6 collective-permute-start.18
  549.1 36.7 %copy-start.13 = (f32[16,16]{1,0:T(8,128)S(1)}, f32[16,16]{1,0:T(8,128)}, u32[]{:S(2)}) copy-start(f32[16,16]{1,0:T(8,128)} %custom-call) | copy-start | bytes 3076
  549.1 61.1 %copy-start.17 = (f32[16,16]{1,0:T(8,128)S(1)}, f32[16,16]{1,0:T(8,128)}, u32[]{:S(2)}) copy-start(f32[16,16]{1,0:T(8,128)} %custom-call.1) | copy-start | bytes 3076
  549.4 96.4 %copy-start.6 = (f32[5,64,2048]{2,1,0:T(8,128)}, f32[5,64,2048]{2,1,0:T(8,128)S(1)}, u32[]{:S(2)}) copy-start(f32[5,64,2048]{2,1,0:T(8,128)S(1)} %add_dynamic-update-slice_fusion) | copy-start | bytes 7864324
  644.8 63.8 %copy-start.12 = (f32[16,16]{1,0:T(8,128)S(1)}, f32[16,16]{1,0:T(8,128)}, u32[]{:S(2)}) copy-start(f32[16,16]{1,0:T(8,128)} %custom-call.2) | copy-start | bytes 3076
  644.8 88.2 %copy-start.16 = (f32[16,16]{1,0:T(8,128)S(1)}, f32[16,16]{1,0:T(8,128)}, u32[]{:S(2)}) copy-start(f32[16,16]{1,0:T(8,128)} %custom-call.3) | copy-start | bytes 3076
  767.6 101.9 %copy-start.11 = (f32[16,16]{1,0:T(8,128)S(1)}, f32[16,16]{1,0:T(8,128)}, u32[]{:S(2)}) copy-start(f32[16,16]{1,0:T(8,128)} %custom-call.4) | copy-start | bytes 3076
  769.9 124.1 %copy-start.15 = (f32[16,16]{1,0:T(8,128)S(1)}, f32[16,16]{1,0:T(8,128)}, u32[]{:S(2)}) copy-start(f32[16,16]{1,0:T(8,128)} %custom-call.5) | copy-start | bytes 3076
  931.3 96.1 %copy-start.10 = (f32[16,16]{1,0:T(8,128)S(1)}, f32[16,16]{1,0:T(8,128)}, u32[]{:S(2)}) copy-start(f32[16,16]{1,0:T(8,128)} %custom-call.6) | copy-start | bytes 3076
  988.9 62.9 %copy-start.14 = (f32[16,16]{1,0:T(8,128)S(1)}, f32[16,16]{1,0:T(8,128)}, u32[]{:S(2)}) copy-start(f32[16,16]{1,0:T(8,128)} %custom-call.7) | copy-start | bytes 3076
  (238 other events, 472.3 us)
